TPU v7x, 256 devices: a whole 4x4x8 slice. The times are simulated.
256 devices in a mesh: expert: 16 (over x_lo, y, core), hidden: 16 (over z, x_hi).
Axes of the slice: x: 4 (x_hi: 2, x_lo: 2; x = x_hi * 2 + x_lo), y: 4, z: 8, core: 2. Of those that a mesh axis runs over, the one named last changes fastest.
Arguments:
- tokens: bfloat16 [4096, 7168], P('expert', 'hidden'), may hold values from -6 to 6
- route_ids: int32 [4096, 2], P('expert'), may hold values from 0 to 15, all different within a row; in each aligned block of 256 rows (0 to 255, 256 to 511, ...) at most 40 rows name the same one
- route_weight: float32 [4096, 2], P('expert'), may hold values from 0.2 to 2
- w_gate: bfloat16 [16, 7168, 2048], P('expert', None, 'hidden'), may hold values from -0.0625 to 0.0625
- w_up: bfloat16 [16, 7168, 2048], P('expert', None, 'hidden'), may hold values from -0.0625 to 0.0625
- w_down: bfloat16 [16, 2048, 7168], P('expert', 'hidden'), may hold values from -0.125 to 0.125
Outputs:
- mixed: bfloat16 [4096, 7168], P('expert', 'hidden')
Inputs may be any that keep to these rules, and one draw needn't show every extreme that they name: `route_ids`: each row names 2 different experts. In the aligned blocks of 256 rows, no expert is named by more than 40 rows of one block, a bound that some block reaches.
All inputs are finite; a program needn't handle non-finite values.
Results may differ from a plain program's by a relative error of at most 0.0057.
Values may be sent and summed in bfloat16 or wider, within the bound.
No kernel may reach another device: no remote copies, remote signals or barrier semaphores. Data moves between devices by JAX's collectives and lax.ppermute only.
A program may use at most 128 MiB of HBM per device.

v0:
```python
import jax
import jax.numpy as jnp
from jax import lax
from jax.sharding import PartitionSpec as P

TOP = 2


def on_device(tokens, route_ids, route_weight, w_gate, w_up, w_down):
    experts = lax.axis_size("expert")
    parts = lax.axis_size("hidden")
    rows_dev, width = tokens.shape
    capacity = (rows_dev * TOP * 5 + 4 * experts - 1) // (4 * experts)
    slot_count = experts * capacity
    matches = route_ids[:, :, None] == jnp.arange(experts, dtype=jnp.int32)[None, None, :]
    chosen = jnp.any(matches, axis=1)
    before = jnp.arange(rows_dev)[:, None] > jnp.arange(rows_dev)[None, :]
    ranking = jnp.dot(
        before.astype(jnp.bfloat16), chosen.astype(jnp.bfloat16), preferred_element_type=jnp.float32
    )
    slot_of = jnp.arange(experts, dtype=jnp.float32)[None, :] * capacity + ranking
    slot_k = jnp.sum(jnp.where(matches, slot_of[:, None, :], 0.0), axis=2).astype(jnp.int32)
    slots = jnp.arange(slot_count, dtype=jnp.int32)
    picks_k = [slot_k[:, k][:, None] == slots[None, :] for k in range(TOP)]
    picks = (picks_k[0] | picks_k[1]).astype(jnp.bfloat16)
    down_w = lax.all_to_all(w_down[0], "hidden", split_axis=1, concat_axis=0, tiled=True)
    leaving = lax.dot_general(
        picks, tokens, (((0,), (0,)), ((), ())), preferred_element_type=jnp.float32
    ).astype(jnp.bfloat16)
    arrived = lax.all_to_all(
        leaving.reshape(experts, capacity, width), "expert", split_axis=0, concat_axis=0, tiled=True
    ).reshape(slot_count, width)
    rows = lax.all_gather(arrived, "hidden", axis=1, tiled=True)
    gate_sum = jnp.dot(rows, w_gate[0], preferred_element_type=jnp.float32)
    up_sum = jnp.dot(rows, w_up[0], preferred_element_type=jnp.float32)
    hidden = (jax.nn.silu(gate_sum) * up_sum).astype(jnp.bfloat16)
    every_hidden = lax.all_gather(hidden, "hidden", axis=1, tiled=True)
    produced = jnp.dot(every_hidden, down_w, preferred_element_type=jnp.float32).astype(
        jnp.bfloat16
    )
    returned = lax.all_to_all(
        produced.reshape(experts, capacity, width),
        "expert",
        split_axis=0,
        concat_axis=0,
        tiled=True,
    ).reshape(slot_count, width)
    mixed = jnp.zeros((rows_dev, width), jnp.float32)
    for k in range(TOP):
        result = jnp.dot(
            picks_k[k].astype(jnp.bfloat16), returned, preferred_element_type=jnp.float32
        )
        mixed = mixed + route_weight[:, k][:, None] * result
    return mixed.astype(jnp.bfloat16)


def solution(mesh):
    in_specs = (
        P("expert", "hidden"),
        P("expert", None),
        P("expert", None),
        P("expert", None, "hidden"),
        P("expert", None, "hidden"),
        P("expert", "hidden", None),
    )
    out_specs = P("expert", "hidden")
    return jax.shard_map(
        on_device, mesh=mesh, in_specs=in_specs, out_specs=out_specs, check_vma=False
    )
```

profile of v0, /device:TPU:1, one launch (start us, length us, event | category | flops | bytes accessed | tf_op | source)
XLA Modules:
  0.0 319.6 jit_solution(8556425088492365411)
XLA Ops:
  6.5 0.0 copy-start
  6.5 0.0 all-gather.3.cloned.1.call-start
  6.5 0.8 fusion.24
  7.4 0.2 convolution_add_fusion
  7.5 0.7 select_reduce_fusion
  8.3 1.5 convolution_convert_fusion
  9.8 0.3 copy.22
  10.1 18.5 %all_to_all.29 = bf16[16,40,448]{2,1,0:T(8,128)(2,1)S(1)} all-to-all(bf16[16,40,448]{2,1,0:T(8,128)(2,1)S(1)} %bitcast.39), channel_id=1, replica_groups=mesh['expert'=16,'hidden'=16] {'expert'}, dimensions={0} | all-to-all | bytes 1146880 | tf_op jit(solution)/shard_map/all_to_all | solution.py:30
  28.5 1.1 copy.23
  29.6 0.0 all-gather.3.cloned.1.call-update
  29.6 0.0 all-gather.5.cloned.1.call-start
  29.7 143.9 %all-gather.3.cloned.1.call-done = bf16[640,7168]{0,1:T(8,128)(2,1)} async-done(((bf16[640,448]{0,1:T(8,128)(2,1)}), bf16[640,7168]{0,1:T(8,128)(2,1)}) %all-gather.3.cloned.1.call-update) | async-done | bytes 9175056 | tf_op jit(solution)/shard_map/all_gather | solution.py:33
  173.6 0.0 copy-done
  173.6 0.0 copy-start.2
  173.6 0.0 copy-start.3
  173.6 6.3 %fusion.5 = f32[640,128]{1,0:T(8,128)S(1)} fusion(bf16[640,7168]{0,1:T(8,128)(2,1)} %all-gather.3.cloned.1.call-done, bf16[1,7168,128]{2,1,0:T(8,128)(2,1)S(1)} %copy-done), kind=kOutput, calls=%fused_computation.5 | convolution fusion | flops 1174405120 | bytes 11337728 | tf_op jit(solution)/shard_map/dot_general | solution.py:34
  179.9 0.0 copy-done.2
  179.9 0.4 copy-done.3
  180.3 3.2 %fusion.15 = bf16[640,128]{1,0:T(8,128)(2,1)} fusion(bf16[640,7168]{0,1:T(8,128)(2,1)S(1)} %copy-done.2, bf16[1,7168,128]{2,1,0:T(8,128)(2,1)S(1)} %copy-done.3, f32[640,128]{1,0:T(8,128)S(1)} %fusion.5), kind=kOutput, calls=%fused_computation.14 | convolution fusion | flops 1174896640 | bytes 11501568 | tf_op jit(solution)/shard_map/dot_general | solution.py:35
  183.6 0.0 all-gather.5.cloned.1.call-update
  183.6 3.9 %copy.24 = bf16[1,128,7168]{1,2,0:T(8,128)(2,1)} copy(bf16[1,128,7168]{2,1,0:T(8,128)(2,1)} %param.11) | data formatting | bytes 3670016 | tf_op args[5]
  187.5 56.4 %all_to_all.30 = bf16[128,16,448]{0,2,1:T(8,128)(2,1)} all-to-all(bf16[128,16,448]{0,2,1:T(8,128)(2,1)} %bitcast.36), channel_id=1, replica_groups=mesh['expert'=16,'hidden'=16] {'hidden'}, dimensions={1} | all-to-all | bytes 3670016 | tf_op jit(solution)/shard_map/all_to_all | solution.py:26
  243.9 42.7 %all-gather.5.cloned.1.call-done = bf16[640,2048]{1,0:T(8,128)(2,1)} async-done(((bf16[640,128]{1,0:T(8,128)(2,1)}), bf16[640,2048]{1,0:T(8,128)(2,1)}) %all-gather.5.cloned.1.call-update) | async-done | bytes 2621456 | tf_op jit(solution)/shard_map/all_gather | solution.py:37
  286.5 3.9 %fusion.7 = bf16[640,448]{0,1:T(8,128)(2,1)S(1)} fusion(bf16[640,2048]{1,0:T(8,128)(2,1)} %all-gather.5.cloned.1.call-done, bf16[128,16,448]{0,2,1:T(8,128)(2,1)} %all_to_all.30), kind=kOutput, calls=%fused_computation.7 | convolution fusion | flops 1174691840 | bytes 5029888 | tf_op jit(solution)/shard_map/dot_general | solution.py:38
  290.4 0.0 copy-start.1
  290.4 1.1 copy.26
  291.5 8.3 %all-to-all-start.2 = ((bf16[16,40,448]{2,1,0:T(8,128)(2,1)}), bf16[16,40,448]{2,1,0:T(8,128)(2,1)S(1)}, u32[]{:S(2)}, u32[]{:S(2)}) async-start(bf16[16,40,448]{2,1,0:T(8,128)(2,1)} %bitcast.9), calls=%async_computation.2 | async-start | bytes 1310720 | tf_op jit(solution)/shard_map/all_to_all | solution.py:41
  299.8 0.0 copy-done.1
  299.8 11.2 %all-to-all-done.2 = bf16[16,40,448]{2,1,0:T(8,128)(2,1)S(1)} async-done(((bf16[16,40,448]{2,1,0:T(8,128)(2,1)}), bf16[16,40,448]{2,1,0:T(8,128)(2,1)S(1)}, u32[]{:S(2)}, u32[]{:S(2)}) %all-to-all-start.2) | async-done | bytes 573472 | tf_op jit(solution)/shard_map/all_to_all | solution.py:41
  311.1 0.5 convolution_multiply_fusion.1
  311.5 1.2 fusion.11
  (4 shorter events, 0.0 us)
Async XLA Ops:
  6.5 167.0 %copy-start = (bf16[1,7168,128]{2,1,0:T(8,128)(2,1)S(1)}, bf16[1,7168,128]{2,1,0:T(8,128)(2,1)}, u32[]{:S(2)}) copy-start(bf16[1,7168,128]{2,1,0:T(8,128)(2,1)} %param.9) | copy-start | bytes 5505028
  6.5 167.0 %all-gather.3.cloned.1.call-start = ((), (), s32[]{:S(2)}) async-start(), calls=%async_computation.3 | async-start | bytes 9748480 | tf_op jit(solution)/shard_map/all_gather | solution.py:33
  29.6 256.9 %all-gather.5.cloned.1.call-start = ((), (), s32[]{:S(2)}) async-start(), calls=%async_computation.4 | async-start | bytes 2785280 | tf_op jit(solution)/shard_map/all_gather | solution.py:37
  173.6 6.3 %copy-start.2 = (bf16[640,7168]{0,1:T(8,128)(2,1)S(1)}, bf16[640,7168]{0,1:T(8,128)(2,1)}, u32[]{:S(2)}) copy-start(bf16[640,7168]{0,1:T(8,128)(2,1)} %all-gather.3.cloned.1.call-done) | copy-start | bytes 27525124
  173.6 6.7 %copy-start.3 = (bf16[1,7168,128]{2,1,0:T(8,128)(2,1)S(1)}, bf16[1,7168,128]{2,1,0:T(8,128)(2,1)}, u32[]{:S(2)}) copy-start(bf16[1,7168,128]{2,1,0:T(8,128)(2,1)} %param.10) | copy-start | bytes 5505028
  290.4 9.4 %copy-start.1 = (f32[256,2]{0,1:T(2,128)S(1)}, f32[256,2]{0,1:T(2,128)}, u32[]{:S(2)}) copy-start(f32[256,2]{0,1:T(2,128)} %param.8) | copy-start | bytes 6148
  291.5 19.5 %all-to-all-start.2 = ((bf16[16,40,448]{2,1,0:T(8,128)(2,1)}), bf16[16,40,448]{2,1,0:T(8,128)(2,1)S(1)}, u32[]{:S(2)}, u32[]{:S(2)}) async-start(bf16[16,40,448]{2,1,0:T(8,128)(2,1)} %bitcast.9), calls=%async_computation.2 | async-start | bytes 1310720 | tf_op jit(solution)/shard_map/all_to_all | solution.py:41
Sparse Core Ops, SparseCore 0:
  29.7 143.7 all-gather.2
  183.7 102.7 all-gather.4
where the time goes:
time: 320 us
  waiting for transfers between devices  198 us (62%)
  blocking collectives  74.9 us (23%)
  matrix products  16.8 us (5%)
  between operations  13.5 us (4%)
  starting transfers between devices  8.31 us (3%)
  local copies, waits for them, and re-layouts  6.73 us (2%)
    all_gather x1, waiting for transfers between devices, on_device(): rows = lax.all_gather(arrived, 'hidden', axis=1, tiled=True)  144 us
    all_to_all x1, blocking collectives, on_device(): lax.all_to_all(w_down[0], 'hidden', split_axis=1, concat_axis=0, tiled=True)  56.4 us
    all_gather x1, waiting for transfers between devices, on_device(): every_hidden = lax.all_gather(hidden, 'hidden', axis=1, tiled=True)  42.7 us
    all_to_all x1, blocking collectives, on_device(): lax.all_to_all(leaving.reshape(experts, capacity, width), 'expert', split...  18.5 us
    all_to_all x1, waiting for transfers between devices, on_device(): lax.all_to_all(produced.reshape(experts, capacity, width), 'expert', spli...  11.2 us
    all_to_all x1, starting transfers between devices, on_device(): lax.all_to_all(produced.reshape(experts, capacity, width), 'expert', spli...  8.26 us
  transfers between devices with their start and end apart: 3, of which 3 were waited for; matrix products, arithmetic and copies ran while one was open for 1% of the time, Pallas kernels for 0%

commit v1 on v0

--- a/solution.py
+++ b/solution.py
@@ -23,7 +23,12 @@
     slots = jnp.arange(slot_count, dtype=jnp.int32)
     picks_k = [slot_k[:, k][:, None] == slots[None, :] for k in range(TOP)]
     picks = (picks_k[0] | picks_k[1]).astype(jnp.bfloat16)
-    down_w = lax.all_to_all(w_down[0], "hidden", split_axis=1, concat_axis=0, tiled=True)
+    down_w = jnp.concatenate(
+        lax.all_to_all(
+            jnp.stack(jnp.split(w_down[0], lax.axis_size("hidden"), axis=1)), "hidden", 0, 0
+        ),
+        axis=0,
+    )
     leaving = lax.dot_general(
         picks, tokens, (((0,), (0,)), ((), ())), preferred_element_type=jnp.float32
     ).astype(jnp.bfloat16)

time: 320 us -> 320 us (level)
  local copies, waits for them, and re-layouts: 6.73 us -> 31.6 us
  waiting for transfers between devices: 198 us -> 174 us
    unnamed x9 -> x24, local copies, waits for them, and re-layouts: 4.29 us -> 27.5 us
    all_gather x1, waiting for transfers between devices: 144 us -> 126 us  [on_device(): rows = lax.all_gather(arrived, 'hidden', axis=1, tiled=True)]
    all_gather x1, waiting for transfers between devices: 42.7 us -> 37.1 us  [on_device(): every_hidden = lax.all_gather(hidden, 'hidden', axis=1, tiled=True)]
  transfers between devices with their start and end apart: 3 -> 3, of which waited for: 3 -> 3; matrix products, arithmetic and copies ran while one was open for 1% -> 9% of each run, Pallas kernels for 0% -> 0%
where the time goes in v1:
time: 320 us; the launch traced here: 319 us
  waiting for transfers between devices  174 us (54%)
  blocking collectives  73.2 us (23%)
  local copies, waits for them, and re-layouts  31.6 us (10%)
  matrix products  16.8 us (5%)
  between operations  13.5 us (4%)
  starting transfers between devices  8.31 us (3%)
    all_gather x1, waiting for transfers between devices, on_device(): rows = lax.all_gather(arrived, 'hidden', axis=1, tiled=True)  126 us
    all_to_all x1, blocking collectives, on_device(): lax.all_to_all(jnp.stack(jnp.split(w_down[0], lax.axis_size('hidden'), ax...  54.7 us
    all_gather x1, waiting for transfers between devices, on_device(): every_hidden = lax.all_gather(hidden, 'hidden', axis=1, tiled=True)  37.1 us
    unnamed x24, local copies, waits for them, and re-layouts  27.5 us
    all_to_all x1, blocking collectives, on_device(): lax.all_to_all(leaving.reshape(experts, capacity, width), 'expert', split...  18.5 us
    all_to_all x1, waiting for transfers between devices, on_device(): lax.all_to_all(produced.reshape(experts, capacity, width), 'expert', spli...  11.2 us
    all_to_all x1, starting transfers between devices, on_device(): lax.all_to_all(produced.reshape(experts, capacity, width), 'expert', spli...  8.27 us
  transfers between devices with their start and end apart: 3, of which 3 were waited for; matrix products, arithmetic and copies ran while one was open for 9% of the time, Pallas kernels for 0%

profile of v1, /device:TPU:1, one launch (start us, length us, event | category | flops | bytes accessed | tf_op | source)
XLA Modules:
  0.0 319.3 jit_solution(10954217773843135116)
XLA Ops:
  6.5 0.0 copy-start
  6.5 0.0 all-gather.3.cloned.1.call-start
  6.5 0.8 fusion.40
  7.4 0.2 convolution_add_fusion
  7.5 0.7 select_reduce_fusion
  8.3 1.5 convolution_convert_fusion
  9.8 0.3 copy.26
  10.1 18.5 %all_to_all.15 = bf16[16,40,448]{2,1,0:T(8,128)(2,1)S(1)} all-to-all(bf16[16,40,448]{2,1,0:T(8,128)(2,1)S(1)} %bitcast.117), channel_id=1, replica_groups=mesh['expert'=16,'hidden'=16] {'expert'}, dimensions={0} | all-to-all | bytes 1146880 | tf_op jit(solution)/shard_map/all_to_all | solution.py:35
  28.5 1.1 copy.27
  29.6 0.0 all-gather.3.cloned.1.call-update
  29.7 0.0 all-gather.5.cloned.1.call-start
  29.7 3.9 %copy.28 = bf16[1,128,7168]{1,2,0:T(8,128)(2,1)} copy(bf16[1,128,7168]{2,1,0:T(8,128)(2,1)} %param.11) | data formatting | bytes 3670016 | tf_op args[5]
  33.6 1.6 fusion.39
  35.2 1.5 fusion.38
  36.7 1.6 fusion.37
  38.3 1.6 fusion.36
  39.8 1.5 fusion.35
  41.4 1.6 fusion.34
  42.9 1.6 fusion.33
  44.5 1.5 fusion.32
  46.0 1.5 fusion.31
  47.6 126.1 %all-gather.3.cloned.1.call-done = bf16[640,7168]{0,1:T(8,128)(2,1)} async-done(((bf16[640,448]{0,1:T(8,128)(2,1)}), bf16[640,7168]{0,1:T(8,128)(2,1)}) %all-gather.3.cloned.1.call-update) | async-done | bytes 9175056 | tf_op jit(solution)/shard_map/all_gather | solution.py:38
  173.6 0.0 copy-done
  173.6 0.0 copy-start.2
  173.6 0.0 copy-start.3
  173.6 6.3 %fusion.5 = f32[640,128]{1,0:T(8,128)S(1)} fusion(bf16[640,7168]{0,1:T(8,128)(2,1)} %all-gather.3.cloned.1.call-done, bf16[1,7168,128]{2,1,0:T(8,128)(2,1)S(1)} %copy-done), kind=kOutput, calls=%fused_computation.5 | convolution fusion | flops 1174405120 | bytes 11337728 | tf_op jit(solution)/shard_map/dot_general | solution.py:39
  180.0 0.0 copy-done.2
  180.0 0.4 copy-done.3
  180.3 3.2 %fusion.15 = bf16[640,128]{1,0:T(8,128)(2,1)} fusion(bf16[640,7168]{0,1:T(8,128)(2,1)S(1)} %copy-done.2, bf16[1,7168,128]{2,1,0:T(8,128)(2,1)S(1)} %copy-done.3, f32[640,128]{1,0:T(8,128)S(1)} %fusion.5), kind=kOutput, calls=%fused_computation.14 | convolution fusion | flops 1174896640 | bytes 11501568 | tf_op jit(solution)/shard_map/dot_general | solution.py:40
  183.6 0.0 all-gather.5.cloned.1.call-update
  183.6 1.5 fusion.30
  185.2 1.6 fusion.29
  186.7 1.6 fusion.28
  188.3 1.5 fusion.27
  189.8 1.6 fusion.26
  191.4 1.5 fusion.25
  192.9 1.6 fusion.24
  194.5 54.7 %all_to_all.16 = bf16[16,128,448]{1,2,0:T(8,128)(2,1)} all-to-all(bf16[16,128,448]{1,2,0:T(8,128)(2,1)} %fusion.24), channel_id=1, replica_groups=mesh['expert'=16,'hidden'=16] {'hidden'}, dimensions={0} | all-to-all | bytes 3670016 | tf_op jit(solution)/shard_map/all_to_all | solution.py:27
  249.2 37.1 %all-gather.5.cloned.1.call-done = bf16[640,2048]{1,0:T(8,128)(2,1)} async-done(((bf16[640,128]{1,0:T(8,128)(2,1)}), bf16[640,2048]{1,0:T(8,128)(2,1)}) %all-gather.5.cloned.1.call-update) | async-done | bytes 2621456 | tf_op jit(solution)/shard_map/all_gather | solution.py:42
  286.3 3.9 %fusion.7 = bf16[640,448]{0,1:T(8,128)(2,1)S(1)} fusion(bf16[640,2048]{1,0:T(8,128)(2,1)} %all-gather.5.cloned.1.call-done, bf16[16,128,448]{1,2,0:T(8,128)(2,1)} %all_to_all.16), kind=kOutput, calls=%fused_computation.7 | convolution fusion | flops 1174691840 | bytes 5029888 | tf_op jit(solution)/shard_map/dot_general | solution.py:43
  290.2 0.0 copy-start.1
  290.2 1.1 copy.30
  291.3 8.3 %all-to-all-start.2 = ((bf16[16,40,448]{2,1,0:T(8,128)(2,1)}), bf16[16,40,448]{2,1,0:T(8,128)(2,1)S(1)}, u32[]{:S(2)}, u32[]{:S(2)}) async-start(bf16[16,40,448]{2,1,0:T(8,128)(2,1)} %bitcast.24), calls=%async_computation.2 | async-start | bytes 1310720 | tf_op jit(solution)/shard_map/all_to_all | solution.py:46
  299.6 0.0 copy-done.1
  299.6 11.2 %all-to-all-done.2 = bf16[16,40,448]{2,1,0:T(8,128)(2,1)S(1)} async-done(((bf16[16,40,448]{2,1,0:T(8,128)(2,1)}), bf16[16,40,448]{2,1,0:T(8,128)(2,1)S(1)}, u32[]{:S(2)}, u32[]{:S(2)}) %all-to-all-start.2) | async-done | bytes 573472 | tf_op jit(solution)/shard_map/all_to_all | solution.py:46
  310.8 0.5 convolution_multiply_fusion.1
  311.3 1.2 fusion.11
  (4 shorter events, 0.0 us)
Async XLA Ops:
  6.5 167.1 %copy-start = (bf16[1,7168,128]{2,1,0:T(8,128)(2,1)S(1)}, bf16[1,7168,128]{2,1,0:T(8,128)(2,1)}, u32[]{:S(2)}) copy-start(bf16[1,7168,128]{2,1,0:T(8,128)(2,1)} %param.9) | copy-start | bytes 5505028
  6.5 167.1 %all-gather.3.cloned.1.call-start = ((), (), s32[]{:S(2)}) async-start(), calls=%async_computation.3 | async-start | bytes 9748480 | tf_op jit(solution)/shard_map/all_gather | solution.py:38
  29.7 256.6 %all-gather.5.cloned.1.call-start = ((), (), s32[]{:S(2)}) async-start(), calls=%async_computation.4 | async-start | bytes 2785280 | tf_op jit(solution)/shard_map/all_gather | solution.py:42
  173.6 6.3 %copy-start.2 = (bf16[640,7168]{0,1:T(8,128)(2,1)S(1)}, bf16[640,7168]{0,1:T(8,128)(2,1)}, u32[]{:S(2)}) copy-start(bf16[640,7168]{0,1:T(8,128)(2,1)} %all-gather.3.cloned.1.call-done) | copy-start | bytes 27525124
  173.6 6.7 %copy-start.3 = (bf16[1,7168,128]{2,1,0:T(8,128)(2,1)S(1)}, bf16[1,7168,128]{2,1,0:T(8,128)(2,1)}, u32[]{:S(2)}) copy-start(bf16[1,7168,128]{2,1,0:T(8,128)(2,1)} %param.10) | copy-start | bytes 5505028
  290.2 9.4 %copy-start.1 = (f32[256,2]{0,1:T(2,128)S(1)}, f32[256,2]{0,1:T(2,128)}, u32[]{:S(2)}) copy-start(f32[256,2]{0,1:T(2,128)} %param.8) | copy-start | bytes 6148
  291.3 19.5 %all-to-all-start.2 = ((bf16[16,40,448]{2,1,0:T(8,128)(2,1)}), bf16[16,40,448]{2,1,0:T(8,128)(2,1)S(1)}, u32[]{:S(2)}, u32[]{:S(2)}) async-start(bf16[16,40,448]{2,1,0:T(8,128)(2,1)} %bitcast.24), calls=%async_computation.2 | async-start | bytes 1310720 | tf_op jit(solution)/shard_map/all_to_all | solution.py:46
Sparse Core Ops, SparseCore 0:
  29.8 143.7 all-gather.2
  183.7 102.5 all-gather.4

commit v2 on v0

--- a/solution.py
+++ b/solution.py
@@ -30,7 +30,9 @@
     arrived = lax.all_to_all(
         leaving.reshape(experts, capacity, width), "expert", split_axis=0, concat_axis=0, tiled=True
     ).reshape(slot_count, width)
-    rows = lax.all_gather(arrived, "hidden", axis=1, tiled=True)
+    rows = jnp.concatenate(
+        lax.all_to_all(jnp.stack([arrived] * lax.axis_size("hidden")), "hidden", 0, 0), axis=1
+    )
     gate_sum = jnp.dot(rows, w_gate[0], preferred_element_type=jnp.float32)
     up_sum = jnp.dot(rows, w_up[0], preferred_element_type=jnp.float32)
     hidden = (jax.nn.silu(gate_sum) * up_sum).astype(jnp.bfloat16)

time: 320 us -> 383 us (1.20)
  blocking collectives: 74.9 us -> 287 us
  waiting for transfers between devices: 198 us -> 53.5 us
    all_to_all x0 -> x1, blocking collectives: none -> 214 us  [on_device(): lax.all_to_all(jnp.stack([arrived] * lax.axis_size('hidden')), 'hidden',...]
    all_gather x1 -> x0, waiting for transfers between devices: 144 us -> none  [on_device(): rows = lax.all_gather(arrived, 'hidden', axis=1, tiled=True)]
  transfers between devices with their start and end apart: 3 -> 2, of which waited for: 3 -> 2; matrix products, arithmetic and copies ran while one was open for 1% -> 1% of each run, Pallas kernels for 0% -> 0%
where the time goes in v2:
time: 383 us
  blocking collectives  287 us (75%)
  waiting for transfers between devices  53.5 us (14%)
  between operations  13.5 us (4%)
  matrix products  13.1 us (3%)
  starting transfers between devices  8.26 us (2%)
  local copies, waits for them, and re-layouts  6.65 us (2%)
    all_to_all x1, blocking collectives, on_device(): lax.all_to_all(jnp.stack([arrived] * lax.axis_size('hidden')), 'hidden',...  214 us
    all_to_all x1, blocking collectives, on_device(): lax.all_to_all(w_down[0], 'hidden', split_axis=1, concat_axis=0, tiled=True)  54.5 us
    all_gather x1, waiting for transfers between devices, on_device(): every_hidden = lax.all_gather(hidden, 'hidden', axis=1, tiled=True)  42.3 us
    all_to_all x1, blocking collectives, on_device(): lax.all_to_all(leaving.reshape(experts, capacity, width), 'expert', split...  18.5 us
    all_to_all x1, waiting for transfers between devices, on_device(): lax.all_to_all(produced.reshape(experts, capacity, width), 'expert', spli...  11.2 us
    all_to_all x1, starting transfers between devices, on_device(): lax.all_to_all(produced.reshape(experts, capacity, width), 'expert', spli...  8.26 us
  transfers between devices with their start and end apart: 2, of which 2 were waited for; matrix products, arithmetic and copies ran while one was open for 1% of the time, Pallas kernels for 0%

profile of v2, /device:TPU:1, one launch (start us, length us, event | category | flops | bytes accessed | tf_op | source)
XLA Modules:
  0.0 383.0 jit_solution(216109219206178962)
XLA Ops:
  6.5 0.0 copy-start
  6.5 0.0 all-gather.2.cloned.1.call-start
  6.5 0.8 fusion.24
  7.4 0.2 convolution_add_fusion
  7.5 0.7 select_reduce_fusion
  8.3 1.5 convolution_convert_fusion
  9.8 0.3 copy.17
  10.1 18.5 %all_to_all.34 = bf16[16,40,448]{2,1,0:T(8,128)(2,1)S(1)} all-to-all(bf16[16,40,448]{2,1,0:T(8,128)(2,1)S(1)} %bitcast.44), channel_id=1, replica_groups=mesh['expert'=16,'hidden'=16] {'expert'}, dimensions={0} | all-to-all | bytes 1146880 | tf_op jit(solution)/shard_map/all_to_all | solution.py:30
  28.5 0.3 copy.18
  28.8 1.1 stack.3
  29.9 213.5 %all_to_all.35 = bf16[16,640,448]{1,2,0:T(8,128)(2,1)S(1)} all-to-all(bf16[16,640,448]{1,2,0:T(8,128)(2,1)S(1)} %stack.3), channel_id=1, replica_groups=mesh['expert'=16,'hidden'=16] {'hidden'}, dimensions={0} | all-to-all | bytes 18350080 | tf_op jit(solution)/shard_map/all_to_all | solution.py:34
  243.4 0.0 copy-done
  243.4 0.0 copy-start.2
  243.4 2.6 fusion.5
  246.0 0.0 copy-done.2
  246.0 3.2 fusion.15
  249.3 0.0 all-gather.2.cloned.1.call-update
  249.3 3.9 %copy.19 = bf16[1,128,7168]{1,2,0:T(8,128)(2,1)} copy(bf16[1,128,7168]{2,1,0:T(8,128)(2,1)} %param.11) | data formatting | bytes 3670016 | tf_op args[5]
  253.2 54.5 %all_to_all.36 = bf16[128,16,448]{0,2,1:T(8,128)(2,1)} all-to-all(bf16[128,16,448]{0,2,1:T(8,128)(2,1)} %bitcast.41), channel_id=1, replica_groups=mesh['expert'=16,'hidden'=16] {'hidden'}, dimensions={1} | all-to-all | bytes 3670016 | tf_op jit(solution)/shard_map/all_to_all | solution.py:26
  307.7 42.3 %all-gather.2.cloned.1.call-done = bf16[640,2048]{1,0:T(8,128)(2,1)} async-done(((bf16[640,128]{1,0:T(8,128)(2,1)}), bf16[640,2048]{1,0:T(8,128)(2,1)}) %all-gather.2.cloned.1.call-update) | async-done | bytes 2621456 | tf_op jit(solution)/shard_map/all_gather | solution.py:39
  350.0 3.9 %fusion.7 = bf16[640,448]{0,1:T(8,128)(2,1)S(1)} fusion(bf16[640,2048]{1,0:T(8,128)(2,1)} %all-gather.2.cloned.1.call-done, bf16[128,16,448]{0,2,1:T(8,128)(2,1)} %all_to_all.36), kind=kOutput, calls=%fused_computation.7 | convolution fusion | flops 1174691840 | bytes 5029888 | tf_op jit(solution)/shard_map/dot_general | solution.py:40
  353.9 0.0 copy-start.1
  353.9 1.1 copy.21
  355.0 8.3 %all-to-all-start.3 = ((bf16[16,40,448]{2,1,0:T(8,128)(2,1)}), bf16[16,40,448]{2,1,0:T(8,128)(2,1)S(1)}, u32[]{:S(2)}, u32[]{:S(2)}) async-start(bf16[16,40,448]{2,1,0:T(8,128)(2,1)} %bitcast.12), calls=%async_computation.3 | async-start | bytes 1310720 | tf_op jit(solution)/shard_map/all_to_all | solution.py:43
  363.3 0.0 copy-done.1
  363.3 11.2 %all-to-all-done.3 = bf16[16,40,448]{2,1,0:T(8,128)(2,1)S(1)} async-done(((bf16[16,40,448]{2,1,0:T(8,128)(2,1)}), bf16[16,40,448]{2,1,0:T(8,128)(2,1)S(1)}, u32[]{:S(2)}, u32[]{:S(2)}) %all-to-all-start.3) | async-done | bytes 573472 | tf_op jit(solution)/shard_map/all_to_all | solution.py:43
  374.5 0.5 convolution_multiply_fusion.1
  375.0 1.2 fusion.11
  (4 shorter events, 0.0 us)
Async XLA Ops:
  6.5 236.9 %copy-start = (bf16[1,7168,128]{2,1,0:T(8,128)(2,1)S(1)}, bf16[1,7168,128]{2,1,0:T(8,128)(2,1)}, u32[]{:S(2)}) copy-start(bf16[1,7168,128]{2,1,0:T(8,128)(2,1)} %param.9) | copy-start | bytes 5505028
  6.5 343.5 %all-gather.2.cloned.1.call-start = ((), (), s32[]{:S(2)}) async-start(), calls=%async_computation.4 | async-start | bytes 2785280 | tf_op jit(solution)/shard_map/all_gather | solution.py:39
  243.4 2.6 copy-start.2
  353.9 9.4 %copy-start.1 = (f32[256,2]{0,1:T(2,128)S(1)}, f32[256,2]{0,1:T(2,128)}, u32[]{:S(2)}) copy-start(f32[256,2]{0,1:T(2,128)} %param.8) | copy-start | bytes 6148
  355.0 19.5 %all-to-all-start.3 = ((bf16[16,40,448]{2,1,0:T(8,128)(2,1)}), bf16[16,40,448]{2,1,0:T(8,128)(2,1)S(1)}, u32[]{:S(2)}, u32[]{:S(2)}) async-start(bf16[16,40,448]{2,1,0:T(8,128)(2,1)} %bitcast.12), calls=%async_computation.3 | async-start | bytes 1310720 | tf_op jit(solution)/shard_map/all_to_all | solution.py:43
Sparse Core Ops, SparseCore 0:
  249.4 100.5 all-gather.1
